TPU v7x, 32 devices: a whole 2x2x4 slice. The times are simulated.
32 devices in a mesh: ctx: 16 (over z, x, core), shard: 2 (over y).
Axes of the slice: x: 2, y: 2, z: 4, core: 2. Of those that a mesh axis runs over, the one named last changes fastest.
Arguments:
- tokens: bfloat16 [2, 4096, 1024], P('shard', 'ctx'), may hold values from -6 to 6
- ln1_gain: bfloat16 [1024], P('shard'), may hold values from 0.25 to 1.75
- ln1_bias: bfloat16 [1024], P('shard'), may hold values from -4 to 4
- qkv_weight: bfloat16 [1024, 3072], P('shard'), may hold values from -0.25 to 0.25
- query_bias: bfloat16 [1024], P('shard'), may hold values from -4 to 4
- value_bias: bfloat16 [1024], P('shard'), may hold values from -4 to 4
- dense_weight: bfloat16 [1024, 1024], P('shard'), may hold values from -0.75 to 0.75
- dense_bias: bfloat16 [1024], P('shard'), may hold values from -4 to 4
- ln2_gain: bfloat16 [1024], P('shard'), may hold values from 0.25 to 1.75
- ln2_bias: bfloat16 [1024], P('shard'), may hold values from -4 to 4
- up_weight: bfloat16 [1024, 4096], P('shard'), may hold values from -0.1875 to 0.1875
- up_bias: bfloat16 [4096], P('shard'), may hold values from -4 to 4
- down_weight: bfloat16 [4096, 1024], P('shard'), may hold values from -0.09375 to 0.09375
- down_bias: bfloat16 [1024], P('shard'), may hold values from -4 to 4
- out_cotangent: bfloat16 [2, 4096, 1024], P('shard', 'ctx'), may hold values from -6 to 6
Outputs:
- block_out: bfloat16 [2, 4096, 1024], P('shard', 'ctx')
- input_grad: bfloat16 [2, 4096, 1024], P('shard', 'ctx')
- ln1_gain_grad: float32 [1024], P('shard')
- ln1_bias_grad: float32 [1024], P('shard')
- qkv_weight_grad: float32 [1024, 3072], P('shard')
- query_bias_grad: float32 [1024], P('shard')
- value_bias_grad: float32 [1024], P('shard')
- dense_weight_grad: float32 [1024, 1024], P('shard')
- dense_bias_grad: float32 [1024], P('shard')
- ln2_gain_grad: float32 [1024], P('shard')
- ln2_bias_grad: float32 [1024], P('shard')
- up_weight_grad: float32 [1024, 4096], P('shard')
- up_bias_grad: float32 [4096], P('shard')
- down_weight_grad: float32 [4096, 1024], P('shard')
- down_bias_grad: float32 [1024], P('shard')
All inputs are finite; a program needn't handle non-finite values.
Results may differ from a plain program's by a relative error of at most 0.023.
Values may be sent and summed in bfloat16 or wider, within the bound.
A program may use at most 320 MiB of HBM per device.

v0:
```python
import jax
import jax.numpy as jnp
from jax import lax
from jax.sharding import PartitionSpec as P

HEADS = 16


neg_large = -1e30
norm_eps = 1e-05


def layer_norm(values, gain_term, bias_term):
    center = values - jnp.mean(values, axis=-1, keepdims=True)
    spread = jnp.mean(center * center, axis=-1, keepdims=True)
    return center * lax.rsqrt(spread + norm_eps) * gain_term + bias_term


def gelu_tanh(values):
    tanh_input = 0.7978845608028654 * (values + 0.044715 * values * values * values)
    return 0.5 * values * (1.0 + jnp.tanh(tanh_input))


def head_slopes(head_count, block_rows, seq_length):
    head_order = jnp.arange(head_count, dtype=jnp.float32)
    fast_rates = 2.0 ** (-head_order) / (4.0 * block_rows)
    slow_rates = 2.0 / seq_length * 2.0 ** (-(head_order - head_count // 2))
    return jnp.where(head_order < head_count // 2, fast_rates, slow_rates)


def block_size(total_rows):
    block_len = min(total_rows, 512)
    while total_rows % block_len:
        block_len -= 1
    return block_len


def score_block(query_rows, key_rows, query_first, key_first, slopes):
    raw_scores = jnp.einsum(
        "sqhe,skhe->shqk", query_rows, key_rows, preferred_element_type=jnp.float32
    )
    raw_scores = raw_scores * query_rows.shape[-1] ** (-0.5)
    query_pos = query_first + jnp.arange(query_rows.shape[1], dtype=jnp.int32)
    key_pos = key_first + jnp.arange(key_rows.shape[1], dtype=jnp.int32)
    distance = (key_pos[None, :] - query_pos[:, None]).astype(jnp.float32)
    allowed = key_pos[None, :] <= query_pos[:, None]
    return (raw_scores + slopes[:, None, None] * distance, allowed)


def score_grads(
    query_rows, grad_rows, log_sums, deltas, query_first, key_rows, value_rows, key_first, slopes
):
    scores, allowed = score_block(query_rows, key_rows, query_first, key_first, slopes)
    weights = jnp.where(allowed, jnp.exp(scores - log_sums[..., None]), 0.0)
    grad_probs = jnp.einsum(
        "sqhe,skhe->shqk", grad_rows, value_rows, preferred_element_type=jnp.float32
    )
    grad_scores = (weights * (grad_probs - deltas[..., None])).astype(jnp.bfloat16)
    return (weights, grad_scores)


def key_block(
    query_rows, grad_rows, log_sums, deltas, query_first, key_rows, value_rows, key_first, slopes
):
    weights, grad_scores = score_grads(
        query_rows,
        grad_rows,
        log_sums,
        deltas,
        query_first,
        key_rows,
        value_rows,
        key_first,
        slopes,
    )
    score_scale = query_rows.shape[-1] ** (-0.5)
    key_grad = (
        jnp.einsum("shqk,sqhe->skhe", grad_scores, query_rows, preferred_element_type=jnp.float32)
        * score_scale
    )
    value_grad = jnp.einsum(
        "shqk,sqhe->skhe",
        weights.astype(jnp.bfloat16),
        grad_rows,
        preferred_element_type=jnp.float32,
    )
    return (key_grad, value_grad)


def forward_fold(queries, query_first, slopes, carried, portion):
    query_last = query_first + queries.shape[1] - 1
    seq_count, head_count, head_dim = (queries.shape[0], queries.shape[2], queries.shape[3])
    key_part, value_part = portion
    block_len = block_size(key_part.shape[1])

    def forward_one_block(block_index, running):
        key_first = block_index * block_len
        key_rows = lax.dynamic_slice_in_dim(
            key_part, block_index * block_len, block_len, 1
        ).reshape(seq_count, block_len, head_count, head_dim)
        value_rows = lax.dynamic_slice_in_dim(
            value_part, block_index * block_len, block_len, 1
        ).reshape(seq_count, block_len, head_count, head_dim)

        def forward_update(current):
            run_max, run_total, run_sum = current
            scores, allowed = score_block(queries, key_rows, query_first, key_first, slopes)
            new_max = jnp.maximum(run_max, jnp.max(jnp.where(allowed, scores, neg_large), axis=-1))
            weights = jnp.where(allowed, jnp.exp(scores - new_max[..., None]), 0.0)
            factor = jnp.exp(run_max - new_max)
            new_total = run_total * factor + jnp.sum(weights, axis=-1)
            block_sum = jnp.einsum(
                "shqk,skhe->sqhe",
                weights.astype(jnp.bfloat16),
                value_rows,
                preferred_element_type=jnp.float32,
            )
            new_sum = run_sum * jnp.transpose(factor, (0, 2, 1))[..., None] + block_sum
            return (new_max, new_total, new_sum)

        return lax.cond(
            key_first <= query_last, forward_update, lambda unchanged: unchanged, running
        )

    return lax.fori_loop(0, key_part.shape[1] // block_len, forward_one_block, carried)


def query_fold(queries, grad_out, log_sums, deltas, query_first, slopes):
    query_last = query_first + queries.shape[1] - 1
    seq_count, head_count, head_dim = (queries.shape[0], queries.shape[2], queries.shape[3])
    score_scale = head_dim ** (-0.5)

    def folded(carried, portion, first_row):
        key_part, value_part = portion
        block_len = block_size(key_part.shape[1])

        def folded_one_block(block_index, running):
            key_first = first_row + block_index * block_len
            key_rows = lax.dynamic_slice_in_dim(
                key_part, block_index * block_len, block_len, 1
            ).reshape(seq_count, block_len, head_count, head_dim)
            value_rows = lax.dynamic_slice_in_dim(
                value_part, block_index * block_len, block_len, 1
            ).reshape(seq_count, block_len, head_count, head_dim)

            def folded_update(current):
                grad_scores = score_grads(
                    queries,
                    grad_out,
                    log_sums,
                    deltas,
                    query_first,
                    key_rows,
                    value_rows,
                    key_first,
                    slopes,
                )[1]
                return (
                    current
                    + jnp.einsum(
                        "shqk,skhe->sqhe", grad_scores, key_rows, preferred_element_type=jnp.float32
                    )
                    * score_scale
                )

            return lax.cond(
                key_first <= query_last, folded_update, lambda unchanged: unchanged, running
            )

        return lax.fori_loop(0, key_part.shape[1] // block_len, folded_one_block, carried)

    return folded


def shards(
    tokens,
    ln1_gain,
    ln1_bias,
    qkv_weight,
    query_bias,
    value_bias,
    dense_weight,
    dense_bias,
    ln2_gain,
    ln2_bias,
    up_weight,
    up_bias,
    down_weight,
    down_bias,
    out_cotangent,
):
    (
        gain_one,
        shift_one,
        weight_qkv,
        bias_query,
        bias_value,
        weight_dense,
        bias_dense,
        gain_two,
        shift_two,
        weight_up,
        bias_up,
        weight_down,
        bias_down,
    ) = (
        lax.all_gather(ln1_gain, "shard", axis=0, tiled=True),
        lax.all_gather(ln1_bias, "shard", axis=0, tiled=True),
        lax.all_gather(qkv_weight, "shard", axis=0, tiled=True),
        lax.all_gather(query_bias, "shard", axis=0, tiled=True),
        lax.all_gather(value_bias, "shard", axis=0, tiled=True),
        lax.all_gather(dense_weight, "shard", axis=0, tiled=True),
        lax.all_gather(dense_bias, "shard", axis=0, tiled=True),
        lax.all_gather(ln2_gain, "shard", axis=0, tiled=True),
        lax.all_gather(ln2_bias, "shard", axis=0, tiled=True),
        lax.all_gather(up_weight, "shard", axis=0, tiled=True),
        lax.all_gather(up_bias, "shard", axis=0, tiled=True),
        lax.all_gather(down_weight, "shard", axis=0, tiled=True),
        lax.all_gather(down_bias, "shard", axis=0, tiled=True),
    )
    seq_count, ctx_rows, width = tokens.shape
    head_count = HEADS
    head_dim = width // head_count
    row_total = seq_count * ctx_rows
    slopes = head_slopes(head_count, ctx_rows, ctx_rows * lax.axis_size("ctx"))
    query_first = lax.axis_index("ctx") * ctx_rows
    head_shape = (seq_count, ctx_rows, head_count, head_dim)
    gain_first = gain_one.astype(jnp.float32)
    shift_first = shift_one.astype(jnp.float32)
    gain_second = gain_two.astype(jnp.float32)
    shift_second = shift_two.astype(jnp.float32)
    inputs = tokens.reshape(row_total, width).astype(jnp.float32)
    normed_low = layer_norm(inputs, gain_first, shift_first).astype(jnp.bfloat16)
    projected = jnp.dot(normed_low, weight_qkv, preferred_element_type=jnp.float32)
    query_low = (
        (projected[:, :width] + bias_query.astype(jnp.float32))
        .astype(jnp.bfloat16)
        .reshape(seq_count, ctx_rows, width)
    )
    key_low = (
        projected[:, width : 2 * width].astype(jnp.bfloat16).reshape(seq_count, ctx_rows, width)
    )
    value_low = (
        (projected[:, 2 * width :] + bias_value.astype(jnp.float32))
        .astype(jnp.bfloat16)
        .reshape(seq_count, ctx_rows, width)
    )
    query_heads = query_low.reshape(head_shape)
    start_state = (
        jnp.full((seq_count, head_count, ctx_rows), neg_large, jnp.float32),
        jnp.zeros((seq_count, head_count, ctx_rows), jnp.float32),
        jnp.zeros(head_shape, jnp.float32),
    )
    run_max, run_total, run_sum = forward_fold(
        query_heads,
        query_first,
        slopes,
        start_state,
        (
            lax.all_gather(key_low, "ctx", axis=1, tiled=True),
            lax.all_gather(value_low, "ctx", axis=1, tiled=True),
        ),
    )
    attended = run_sum / jnp.transpose(run_total, (0, 2, 1))[..., None]
    log_sums = run_max + jnp.log(run_total)
    attended_flat = attended.reshape(row_total, width)
    attended_low = attended_flat.astype(jnp.bfloat16)
    middle = (
        inputs
        + jnp.dot(attended_low, weight_dense, preferred_element_type=jnp.float32)
        + bias_dense.astype(jnp.float32)
    )
    normed_two_low = layer_norm(middle, gain_second, shift_second).astype(jnp.bfloat16)
    hidden = jnp.dot(
        normed_two_low, weight_up, preferred_element_type=jnp.float32
    ) + bias_up.astype(jnp.float32)
    active_low = gelu_tanh(hidden).astype(jnp.bfloat16)
    outputs = (
        middle
        + jnp.dot(active_low, weight_down, preferred_element_type=jnp.float32)
        + bias_down.astype(jnp.float32)
    )
    block_out = outputs.astype(jnp.bfloat16).reshape(tokens.shape)
    grad_out_low = out_cotangent.reshape(row_total, width)
    grad_outputs = grad_out_low.astype(jnp.float32)
    grad_down_weight = jnp.einsum(
        "rf,rd->fd", active_low, grad_out_low, preferred_element_type=jnp.float32
    )
    grad_down_bias = jnp.sum(grad_outputs, axis=0)
    grad_active = jnp.einsum(
        "rd,fd->rf", grad_out_low, weight_down, preferred_element_type=jnp.float32
    )
    grad_hidden_low = jax.vjp(gelu_tanh, hidden)[1](grad_active)[0].astype(jnp.bfloat16)
    grad_up_weight = jnp.einsum(
        "rd,rf->df", normed_two_low, grad_hidden_low, preferred_element_type=jnp.float32
    )
    grad_up_bias = jnp.sum(grad_hidden_low.astype(jnp.float32), axis=0)
    grad_normed_two = jnp.einsum(
        "rf,df->rd", grad_hidden_low, weight_up, preferred_element_type=jnp.float32
    )
    norm_back_two = jax.vjp(layer_norm, middle, gain_second, shift_second)[1]
    grad_middle_norm, grad_gain_two, grad_shift_two = norm_back_two(grad_normed_two)
    grad_middle = grad_outputs + grad_middle_norm
    grad_dense_low = grad_middle.astype(jnp.bfloat16)
    grad_dense_weight = jnp.einsum(
        "rd,re->de", attended_low, grad_dense_low, preferred_element_type=jnp.float32
    )
    grad_dense_bias = jnp.sum(grad_dense_low.astype(jnp.float32), axis=0)
    grad_attended_low = jnp.einsum(
        "re,de->rd", grad_dense_low, weight_dense, preferred_element_type=jnp.float32
    ).astype(jnp.bfloat16)
    deltas_rows = jnp.sum(
        (grad_attended_low.astype(jnp.float32) * attended_flat).reshape(head_shape), axis=-1
    )
    deltas = jnp.transpose(deltas_rows, (0, 2, 1))
    grad_heads = grad_attended_low.reshape(head_shape)
    zero_heads = jnp.zeros(head_shape, jnp.float32)
    query_last = query_first + ctx_rows - 1
    key_all = lax.all_gather(key_low[0], "ctx", axis=0, tiled=True)
    value_all = lax.all_gather(value_low[0], "ctx", axis=0, tiled=True)
    fold_one = query_fold(query_heads, grad_heads, log_sums, deltas, query_first, slopes)
    query_parts = fold_one(zero_heads, (key_all[None], value_all[None]), 0)
    row_count = ctx_rows * lax.axis_size("ctx")
    block_len = block_size(row_count)

    def key_one_block(block_index):
        key_start = block_index * block_len
        key_rows = lax.dynamic_slice_in_dim(key_all, key_start, block_len, 0).reshape(
            1, block_len, head_count, head_dim
        )
        value_rows = lax.dynamic_slice_in_dim(value_all, key_start, block_len, 0).reshape(
            1, block_len, head_count, head_dim
        )

        def compute(unused):
            key_grad, value_grad = key_block(
                query_heads,
                grad_heads,
                log_sums,
                deltas,
                query_first,
                key_rows,
                value_rows,
                key_start,
                slopes,
            )
            return jnp.concatenate(
                [key_grad.reshape(block_len, width), value_grad.reshape(block_len, width)], axis=1
            )

        def skipped(unused):
            return jnp.zeros((block_len, 2 * width), jnp.float32)

        return lax.cond(key_start <= query_last, compute, skipped, 0)

    blocks = lax.map(key_one_block, jnp.arange(row_count // block_len, dtype=jnp.int32))
    pair_grads = lax.psum_scatter(
        blocks.reshape(row_count, 2 * width).astype(jnp.bfloat16),
        "ctx",
        scatter_dimension=0,
        tiled=True,
    ).astype(jnp.float32)
    key_parts = [pair_grads[:, :width]]
    value_parts = [pair_grads[:, width:]]
    grad_key = jnp.stack(key_parts).reshape(head_shape)
    grad_value = jnp.stack(value_parts).reshape(head_shape)
    grad_qkv_low = jnp.concatenate(
        [
            query_parts.reshape(row_total, width),
            grad_key.reshape(row_total, width),
            grad_value.reshape(row_total, width),
        ],
        axis=1,
    ).astype(jnp.bfloat16)
    grad_qkv_weight = jnp.einsum(
        "rd,rc->dc", normed_low, grad_qkv_low, preferred_element_type=jnp.float32
    )
    grad_query_bias = jnp.sum(grad_qkv_low[:, :width].astype(jnp.float32), axis=0)
    grad_value_bias = jnp.sum(grad_qkv_low[:, 2 * width :].astype(jnp.float32), axis=0)
    grad_normed_one = jnp.einsum(
        "rc,dc->rd", grad_qkv_low, weight_qkv, preferred_element_type=jnp.float32
    )
    norm_back_one = jax.vjp(layer_norm, inputs, gain_first, shift_first)[1]
    grad_input_norm, grad_gain_one, grad_shift_one = norm_back_one(grad_normed_one)
    input_grad = (grad_middle + grad_input_norm).astype(jnp.bfloat16).reshape(tokens.shape)
    (
        part_gain_one,
        part_shift_one,
        part_qkv,
        part_query,
        part_value,
        part_dense,
        part_dense_bias,
        part_gain_two,
        part_shift_two,
        part_up,
        part_up_bias,
        part_down,
        part_down_bias,
    ) = (
        lax.psum_scatter(
            grad_gain_one.astype(jnp.bfloat16), "shard", scatter_dimension=0, tiled=True
        ).astype(jnp.float32),
        lax.psum_scatter(
            grad_shift_one.astype(jnp.bfloat16), "shard", scatter_dimension=0, tiled=True
        ).astype(jnp.float32),
        lax.psum_scatter(
            grad_qkv_weight.astype(jnp.bfloat16), "shard", scatter_dimension=0, tiled=True
        ).astype(jnp.float32),
        lax.psum_scatter(
            grad_query_bias.astype(jnp.bfloat16), "shard", scatter_dimension=0, tiled=True
        ).astype(jnp.float32),
        lax.psum_scatter(
            grad_value_bias.astype(jnp.bfloat16), "shard", scatter_dimension=0, tiled=True
        ).astype(jnp.float32),
        lax.psum_scatter(
            grad_dense_weight.astype(jnp.bfloat16), "shard", scatter_dimension=0, tiled=True
        ).astype(jnp.float32),
        lax.psum_scatter(
            grad_dense_bias.astype(jnp.bfloat16), "shard", scatter_dimension=0, tiled=True
        ).astype(jnp.float32),
        lax.psum_scatter(
            grad_gain_two.astype(jnp.bfloat16), "shard", scatter_dimension=0, tiled=True
        ).astype(jnp.float32),
        lax.psum_scatter(
            grad_shift_two.astype(jnp.bfloat16), "shard", scatter_dimension=0, tiled=True
        ).astype(jnp.float32),
        lax.psum_scatter(
            grad_up_weight.astype(jnp.bfloat16), "shard", scatter_dimension=0, tiled=True
        ).astype(jnp.float32),
        lax.psum_scatter(
            grad_up_bias.astype(jnp.bfloat16), "shard", scatter_dimension=0, tiled=True
        ).astype(jnp.float32),
        lax.psum_scatter(
            grad_down_weight.astype(jnp.bfloat16), "shard", scatter_dimension=0, tiled=True
        ).astype(jnp.float32),
        lax.psum_scatter(
            grad_down_bias.astype(jnp.bfloat16), "shard", scatter_dimension=0, tiled=True
        ).astype(jnp.float32),
    )
    totals = (
        lax.psum(part_gain_one.astype(jnp.bfloat16), "ctx").astype(jnp.float32),
        lax.psum(part_shift_one.astype(jnp.bfloat16), "ctx").astype(jnp.float32),
        lax.psum(part_qkv.astype(jnp.bfloat16), "ctx").astype(jnp.float32),
        lax.psum(part_query.astype(jnp.bfloat16), "ctx").astype(jnp.float32),
        lax.psum(part_value.astype(jnp.bfloat16), "ctx").astype(jnp.float32),
        lax.psum(part_dense.astype(jnp.bfloat16), "ctx").astype(jnp.float32),
        lax.psum(part_dense_bias.astype(jnp.bfloat16), "ctx").astype(jnp.float32),
        lax.psum(part_gain_two.astype(jnp.bfloat16), "ctx").astype(jnp.float32),
        lax.psum(part_shift_two.astype(jnp.bfloat16), "ctx").astype(jnp.float32),
        lax.psum(part_up.astype(jnp.bfloat16), "ctx").astype(jnp.float32),
        lax.psum(part_up_bias.astype(jnp.bfloat16), "ctx").astype(jnp.float32),
        lax.psum(part_down.astype(jnp.bfloat16), "ctx").astype(jnp.float32),
        lax.psum(part_down_bias.astype(jnp.bfloat16), "ctx").astype(jnp.float32),
    )
    return (block_out, input_grad) + tuple(totals)


def solution(mesh):
    return jax.shard_map(
        shards,
        mesh=mesh,
        in_specs=(
            P("shard", "ctx", None),
            P("shard"),
            P("shard"),
            P("shard", None),
            P("shard"),
            P("shard"),
            P("shard", None),
            P("shard"),
            P("shard"),
            P("shard"),
            P("shard", None),
            P("shard"),
            P("shard", None),
            P("shard"),
            P("shard", "ctx", None),
        ),
        out_specs=(
            P("shard", "ctx", None),
            P("shard", "ctx", None),
            P("shard"),
            P("shard"),
            P("shard", None),
            P("shard"),
            P("shard"),
            P("shard", None),
            P("shard"),
            P("shard"),
            P("shard"),
            P("shard", None),
            P("shard"),
            P("shard", None),
            P("shard"),
        ),
        check_vma=False,
    )
```

profile of v0, /device:TPU:0, one launch (start us, length us, event | category | flops | bytes accessed | tf_op | source)
XLA Modules:
  0.0 1530.4 jit_solution(2776308289016824116)
XLA Ops:
  8.7 5.2 all-gather.2
  14.6 4.3 all-gather.3
  21.7 71.0 %all-gather.17.cloned.1.call-done = bf16[1024,3072]{1,0:T(8,128)(2,1)} async-done(((bf16[512,3072]{1,0:T(8,128)(2,1)}), bf16[1024,3072]{1,0:T(8,128)(2,1)}) %all-gather.17.cloned.1.call-update) | async-done | bytes 6291472 | tf_op jit(solution)/shard_map/all_gather | solution.py:209
  92.7 4.7 fusion.116
  100.1 4.3 all-gather.4
  104.4 4.3 all-gather.5
  108.8 2.7 fusion.99
  113.4 4.3 all-gather.6
  117.7 4.3 all-gather.7
  122.1 4.3 all-gather.8
  126.4 4.6 all_gather.63
  131.3 43.8 %all-gather.25.cloned.1.call-done = bf16[4096,1024]{1,0:T(8,128)(2,1)} async-done(((bf16[256,1024]{1,0:T(8,128)(2,1)}), bf16[4096,1024]{1,0:T(8,128)(2,1)}) %all-gather.25.cloned.1.call-update) | async-done | bytes 8388624 | tf_op jit(solution)/shard_map/all_gather | solution.py:260
  175.1 12.0 copy.80
  187.0 63.9 %all-gather.27.cloned.1.call-done = bf16[4096,1024]{1,0:T(8,128)(2,1)} async-done(((bf16[256,1024]{1,0:T(8,128)(2,1)}), bf16[4096,1024]{1,0:T(8,128)(2,1)}) %all-gather.27.cloned.1.call-update) | async-done | bytes 8388624 | tf_op jit(solution)/shard_map/all_gather | solution.py:261
  251.0 12.0 copy.81
  263.1 10.2 while.46
  263.1 9.6 conditional.9
  265.2 2.8 select_reduce_fusion
  270.3 2.4 fusion.7
  274.7 9.1 all-gather.19.cloned.1.call-done
  283.8 2.4 fusion.126
  286.5 102.7 %all-gather.21.cloned.1.call-done = bf16[1024,4096]{1,0:T(8,128)(2,1)} async-done(((bf16[512,4096]{1,0:T(8,128)(2,1)}), bf16[1024,4096]{1,0:T(8,128)(2,1)}) %all-gather.21.cloned.1.call-update) | async-done | bytes 8388624 | tf_op jit(solution)/shard_map/all_gather | solution.py:216
  389.2 7.9 convolution_add_fusion
  397.1 97.6 %all-gather.23.cloned.1.call-done = bf16[4096,1024]{1,0:T(8,128)(2,1)} async-done(((bf16[2048,1024]{1,0:T(8,128)(2,1)}), bf16[4096,1024]{1,0:T(8,128)(2,1)}) %all-gather.23.cloned.1.call-update) | async-done | bytes 8388624 | tf_op jit(solution)/shard_map/all_gather | solution.py:218
  494.7 9.9 fusion.127
  504.6 3.2 multiply_reduce_fusion
  514.0 11.2 copy.87
  525.3 11.5 copy.88
  536.8 79.8 %while.48 = (s32[]{:T(128)}, bf16[8,512,2048]{2,1,0:T(8,128)(2,1)}, s32[8]{0:T(128)S(1)}, s32[]{:T(128)}, s32[]{:T(128)}, /*index=5*/bf16[4096,1024]{0,1:T(8,128...) while((s32[]{:T(128)}, bf16[8,512,2048]{2,1,0:T(8,128)(2,1)}, ...), condition=%wide.region_20.21_spmd.clone, body=%wide.region_17.0_spmd.clone.sunk | while | flops 1108738944 | bytes 62842896 | solution.py:356
  538.2 22.4 %conditional.11 = (bf16[1,512,2048]{1,2,0:T(8,128)(2,1)S(1)}) conditional(s32[]{:T(128)} %convert_element_type.423, () %tuple.231, (s32[]{:T(128)}, s32[]{:T(128)}, bf16[4096,1024]{0,1:T(8,128)(2,1)}, bf16[1,256,16,64]{1,3,2,0:T(8,128)(2,1)S(1)}, f32[16]{0:T(128)S(1)}, /*index=5*/f32[1,16,256]{2,1,0:T(8,128)S(1)}, ...), branch_computations={%region_18.18_spmd, %region_19.19_spmd.clone} | conditional | flops 1108738944 | bytes 46065236 | solution.py:354
  538.3 2.8 constant_dynamic-slice_fusion.4
  541.4 4.5 fusion.67
  545.9 8.8 fusion.60
  554.7 5.8 fusion.53
  562.0 2.9 copy.111
  569.2 2.9 copy.111
  576.3 2.9 copy.111
  583.5 2.9 copy.111
  590.7 2.9 copy.111
  597.9 2.9 copy.111
  605.1 2.9 copy.111
  612.2 2.9 copy.111
  620.2 8.4 convolution_convert_fusion
  629.9 7.3 convolution_convert_fusion.1
  638.4 16.7 %while.47 = (s32[]{:T(128)}, f32[1,256,16,64]{1,3,2,0:T(8,128)}, s32[]{:T(128)}, bf16[1,4096,1024]{1,2,0:T(8,128)(2,1)}, s32[]{:T(128)}, /*index=5*/bf16[1,256,1...) while((s32[]{:T(128)}, f32[1,256,16,64]{1,3,2,0:T(8,128)}, ...), condition=%wide.region_16.17_spmd.clone, body=%wide.region_13.0_spmd.clone.sunk | while | flops 823001984 | bytes 28616576 | solution.py:170
  638.4 16.3 %conditional.10 = (f32[1,256,16,64]{1,3,2,0:T(8,128)}) conditional(s32[]{:T(128)} %convert_element_type.422, f32[1,256,16,64]{1,3,2,0:T(8,128)} %get-tuple-element.1536, (s32[]{:T(128)}, bf16[1,4096,1024]{1,2,0:T(8,128)(2,1)}, s32[]{:T(128)}, bf16[1,256,16,64]{1,3,2,0:T(8,128)(2,1)S(1)}, f32[16]{0:T(128)S(1)}, ...), branch_computations={%region_14.14_spmd, %region_15.15_spmd.clone} | conditional | flops 823001984 | bytes 28616182 | solution.py:166
  641.3 4.5 fusion.42
  645.8 8.9 fusion.37
  656.8 294.5 %reduce-scatter.6.cloned.1.call-done = bf16[256,2048]{1,0:T(8,128)(2,1)} async-done(((bf16[4096,2048]{1,0:T(8,128)(2,1)}), bf16[256,2048]{1,0:T(8,128)(2,1)}) %reduce-scatter.6.cloned.1.call-update) | async-done | bytes 1048592 | tf_op jit(solution)/shard_map/reduce_scatter | solution.py:357
  951.3 5.9 convolution_convert_fusion.2
  957.3 27.6 %reduce-scatter.10.cloned.1.call-done = bf16[512,1024]{1,0:T(8,128)(2,1)} async-done(((bf16[1024,1024]{1,0:T(8,128)(2,1)}), bf16[512,1024]{1,0:T(8,128)(2,1)}) %reduce-scatter.10.cloned.1.call-update) | async-done | bytes 1048592 | tf_op jit(solution)/shard_map/reduce_scatter | solution.py:416
  985.0 101.7 %reduce-scatter.14.cloned.1.call-done = bf16[2048,1024]{1,0:T(8,128)(2,1)} async-done(((bf16[4096,1024]{1,0:T(8,128)(2,1)}), bf16[2048,1024]{1,0:T(8,128)(2,1)}) %reduce-scatter.14.cloned.1.call-update) | async-done | bytes 4194320 | tf_op jit(solution)/shard_map/reduce_scatter | solution.py:434
  1086.7 101.4 %reduce-scatter.12.cloned.1.call-done = bf16[512,4096]{1,0:T(8,128)(2,1)} async-done(((bf16[1024,4096]{1,0:T(8,128)(2,1)}), bf16[512,4096]{1,0:T(8,128)(2,1)}) %reduce-scatter.12.cloned.1.call-update) | async-done | bytes 4194320 | tf_op jit(solution)/shard_map/reduce_scatter | solution.py:428
  1188.1 80.1 %reduce-scatter.8.cloned.1.call-done = bf16[512,3072]{1,0:T(8,128)(2,1)} async-done(((bf16[1024,3072]{1,0:T(8,128)(2,1)}), bf16[512,3072]{1,0:T(8,128)(2,1)}) %reduce-scatter.8.cloned.1.call-update) | async-done | bytes 3145744 | tf_op jit(solution)/shard_map/reduce_scatter | solution.py:407
  1270.7 4.6 all-gather.9
  1275.5 9.1 fusion.91
  1284.8 4.9 fusion.121
  1290.3 7.0 all-reduce.11
  1297.9 62.4 %all-reduce.9 = (bf16[512]{0:T(512)(128)(2,1)S(1)}, bf16[512]{0:T(512)(128)(2,1)S(1)}, bf16[512]{0:T(512)(128)(2,1)S(1)}, bf16[512]{0:T(512)(128)(2,1)S(1)}, bf1...) all-reduce(bf16[512]{0:T(512)(128)(2,1)S(1)} %dynamic-slice.1, ...), channel_id=1, replica_groups=mesh['ctx'=16,'shard'=2] {'ctx'}, use_global_device_ids=true, to_apply=%region_26.27 | all-reduce | flops 6144 | bytes 24576 | tf_op jit(solution)/shard_map/psum | solution.py:442
  1366.8 141.1 %all-reduce.14.cloned.1.call-done = (bf16[512,3072]{1,0:T(8,128)(2,1)}, bf16[512,1024]{1,0:T(8,128)(2,1)}, bf16[512,4096]{1,0:T(8,128)(2,1)}, bf16[2048,1024]{1,0:T(8,128)(2,1)}) async-done(((bf16[512,3072]{1,0:T(8,128)(2,1)}, bf16[512,1024]{1,0:T(8,128)(2,1)}, bf16[512,4096]{1,0:T(8,128)(2,1)}, bf16[2048,1024]{1,0:T(8,128)(2,1)}), (bf16[512,3072]{1,0:T(8,128)(2,1)}, bf16[512,1024]{1,0:T(8,128)(2,1)}, ...) | async-done | bytes 12582928 | tf_op jit(solution)/shard_map/psum | solution.py:444
  1507.9 2.9 convert_element_type.289
  1510.8 3.5 convert_element_type.285
  1514.4 4.5 convert_element_type.296
  1518.8 4.4 convert_element_type.299
  (322 shorter events, 71.6 us)
Async XLA Ops:
  7.2 85.5 %copy-start.2 = (bf16[1,256,1024]{2,1,0:T(8,128)(2,1)S(1)}, bf16[1,256,1024]{2,1,0:T(8,128)(2,1)}, u32[]{:S(2)}) copy-start(bf16[1,256,1024]{2,1,0:T(8,128)(2,1)} %param.27) | copy-start | bytes 1572868
  7.2 85.5 %all-gather.17.cloned.1.call-start = ((), (), s32[]{:S(2)}) async-start(), calls=%async_computation.5 | async-start | bytes 9437184 | tf_op jit(solution)/shard_map/all_gather | solution.py:209
  7.9 167.1 %all-gather.25.cloned.1.call-start = ((), (), s32[]{:S(2)}) async-start(), calls=%async_computation.14 | async-start | bytes 8912896 | tf_op jit(solution)/shard_map/all_gather | solution.py:260
  13.9 83.5 %copy-start.24 = (f32[2,1,512]{2,1,0:T(1,128)}, f32[2,1,512]{2,1,0:T(1,128)S(1)}, u32[]{:S(2)}) copy-start(f32[2,1,512]{2,1,0:T(1,128)S(1)} %convert_element_type.301) | copy-start | bytes 12292
  18.9 78.5 %copy-start.26 = (f32[2,1,512]{2,1,0:T(1,128)}, f32[2,1,512]{2,1,0:T(1,128)S(1)}, u32[]{:S(2)}) copy-start(f32[2,1,512]{2,1,0:T(1,128)S(1)} %convert_element_type.302) | copy-start | bytes 12292
  20.2 77.2 %copy-start.28 = (f32[256]{0:T(256)}, f32[256]{0:T(256)S(1)}, u32[]{:S(2)}) copy-start(f32[256]{0:T(256)S(1)} %broadcast_multiply_fusion.1) | copy-start | bytes 3076
  21.6 75.8 %copy-start.32 = (f32[256]{0:T(256)}, f32[256]{0:T(256)S(1)}, u32[]{:S(2)}) copy-start(f32[256]{0:T(256)S(1)} %fusion.97) | copy-start | bytes 3076
  21.7 75.8 %copy-start.30 = (f32[256]{0:T(256)}, f32[256]{0:T(256)S(1)}, u32[]{:S(2)}) copy-start(f32[256]{0:T(256)S(1)} %fusion.111) | copy-start | bytes 3076
  92.7 7.4 copy-start.41
  92.7 11.7 copy-start.42
  97.5 1.7 copy-start.20
  100.0 151.0 %all-gather.27.cloned.1.call-start = ((), (), s32[]{:S(2)}) async-start(), calls=%async_computation.15 | async-start | bytes 8912896 | tf_op jit(solution)/shard_map/all_gather | solution.py:261
  111.5 172.3 %all-gather.19.cloned.1.call-start = ((), (), s32[]{:S(2)}) async-start(), calls=%async_computation.6 | async-start | bytes 3145728 | tf_op jit(solution)/shard_map/all_gather | solution.py:212
  112.1 1.3 copy-start.43
  112.1 5.6 copy-start.44
  112.1 10.0 copy-start.45
  112.1 14.3 copy-start.38
  112.1 277.1 %all-gather.21.cloned.1.call-start = ((), (), s32[]{:S(2)}) async-start(), calls=%async_computation.7 | async-start | bytes 12582912 | tf_op jit(solution)/shard_map/all_gather | solution.py:216
  112.7 382.0 %all-gather.23.cloned.1.call-start = ((), (), s32[]{:S(2)}) async-start(), calls=%async_computation.8 | async-start | bytes 12582912 | tf_op jit(solution)/shard_map/all_gather | solution.py:218
  113.3 838.0 %reduce-scatter.6.cloned.1.call-start = ((), (), s32[]{:S(2)}) async-start(), calls=%async_computation.9 | async-start | bytes 17825792 | tf_op jit(solution)/shard_map/reduce_scatter | solution.py:357
  273.4 123.7 %copy-start.7 = (f32[1,256,16,64]{1,3,2,0:T(8,128)}, f32[1,256,16,64]{1,3,2,0:T(8,128)S(1)}, u32[]{:S(2)}) copy-start(f32[1,256,16,64]{1,3,2,0:T(8,128)S(1)} %broadcast_divide_fusion) | copy-start | bytes 3145732
  286.2 221.6 %copy-start.4 = (f32[256,1024]{1,0:T(8,128)}, f32[256,1024]{1,0:T(8,128)S(1)}, u32[]{:S(2)}) copy-start(f32[256,1024]{1,0:T(8,128)S(1)} %get-tuple-element.1242) | copy-start | bytes 3145732
  389.2 105.5 %copy-start.12 = (bf16[1,256,1024]{2,1,0:T(8,128)(2,1)S(1)}, bf16[1,256,1024]{2,1,0:T(8,128)(2,1)}, u32[]{:S(2)}) copy-start(bf16[1,256,1024]{2,1,0:T(8,128)(2,1)} %param.41) | copy-start | bytes 1572868
  494.7 9.9 copy-start.47
  504.6 3.2 copy-start.21
  507.8 2.2 copy-start.11
  507.8 2.2 copy-start.17
  508.2 3.7 copy-start.34
  554.7 5.8 copy-start.1
  560.7 1.3 copy-start
  567.9 1.3 copy-start
  575.0 1.3 copy-start
  582.2 1.3 copy-start
  589.4 1.3 copy-start
  596.6 1.3 copy-start
  603.8 1.3 copy-start
  610.9 1.3 copy-start
  616.7 3.5 copy-start.13
  616.7 368.3 %reduce-scatter.10.cloned.1.call-start = ((), (), s32[]{:S(2)}) async-start(), calls=%async_computation.11 | async-start | bytes 3145728 | tf_op jit(solution)/shard_map/reduce_scatter | solution.py:416
  619.9 466.7 %reduce-scatter.14.cloned.1.call-start = ((), (), s32[]{:S(2)}) async-start(), calls=%async_computation.13 | async-start | bytes 12582912 | tf_op jit(solution)/shard_map/reduce_scatter | solution.py:434
  628.7 559.4 %reduce-scatter.12.cloned.1.call-start = ((), (), s32[]{:S(2)}) async-start(), calls=%async_computation.12 | async-start | bytes 12582912 | tf_op jit(solution)/shard_map/reduce_scatter | solution.py:428
  637.2 630.9 %reduce-scatter.8.cloned.1.call-start = ((), (), s32[]{:S(2)}) async-start(), calls=%async_computation.10 | async-start | bytes 9437184 | tf_op jit(solution)/shard_map/reduce_scatter | solution.py:407
  638.4 312.9 %copy-start.3 = (bf16[1,256,1024]{2,1,0:T(8,128)(2,1)S(1)}, bf16[1,256,1024]{2,1,0:T(8,128)(2,1)}, u32[]{:S(2)}) copy-start(bf16[1,256,1024]{2,1,0:T(8,128)(2,1)} %param.27) | copy-start | bytes 1572868
  638.4 312.9 %copy-start.25 = (f32[2,1,512]{2,1,0:T(1,128)S(1)}, f32[2,1,512]{2,1,0:T(1,128)}, u32[]{:S(2)}) copy-start(f32[2,1,512]{2,1,0:T(1,128)} %copy-done.24) | copy-start | bytes 12292
  638.4 312.9 %copy-start.27 = (f32[2,1,512]{2,1,0:T(1,128)S(1)}, f32[2,1,512]{2,1,0:T(1,128)}, u32[]{:S(2)}) copy-start(f32[2,1,512]{2,1,0:T(1,128)} %copy-done.26) | copy-start | bytes 12292
  638.4 312.9 %copy-start.29 = (f32[256]{0:T(256)S(1)}, f32[256]{0:T(256)}, u32[]{:S(2)}) copy-start(f32[256]{0:T(256)} %copy-done.28) | copy-start | bytes 3076
  638.4 312.9 %copy-start.31 = (f32[256]{0:T(256)S(1)}, f32[256]{0:T(256)}, u32[]{:S(2)}) copy-start(f32[256]{0:T(256)} %copy-done.30) | copy-start | bytes 3076
  656.8 300.4 %copy-start.22 = (bf16[256,1024]{1,0:T(8,128)(2,1)}, bf16[256,1024]{1,0:T(8,128)(2,1)S(1)}, u32[]{:S(2)}) copy-start(bf16[256,1024]{1,0:T(8,128)(2,1)S(1)} %copy.90) | copy-start | bytes 1572868
  957.3 550.6 %all-reduce.14.cloned.1.call-start = ((), (), s32[]{:S(2)}) async-start(), calls=%async_computation.16 | async-start | bytes 25165824 | tf_op jit(solution)/shard_map/psum | solution.py:444
  1268.2 2.5 copy-start.46
  1268.2 7.2 copy-start.14
  1268.2 7.3 copy-start.6
  1275.5 9.1 copy-start.19
  1275.5 9.2 copy-start.23
  1284.7 5.0 copy-start.33
  1284.7 5.6 copy-start.36
  1284.7 5.6 copy-start.37
  1284.7 5.6 copy-start.39
  1284.7 5.6 copy-start.40
  1284.8 80.8 %copy-start.10 = (f32[256,1024]{1,0:T(8,128)S(1)}, f32[256,1024]{1,0:T(8,128)}, u32[]{:S(2)}) copy-start(f32[256,1024]{1,0:T(8,128)} %copy-done.9) | copy-start | bytes 3145732
  1284.8 80.8 %copy-start.35 = (f32[256]{0:T(256)S(1)}, f32[256]{0:T(256)}, u32[]{:S(2)}) copy-start(f32[256]{0:T(256)} %copy-done.34) | copy-start | bytes 3076
  1507.9 2.9 copy-start.18
  1510.8 3.5 copy-start.16
  1514.4 4.5 copy-start.15
  (4 other events, 4.1 us)
Sparse Core Ops, SparseCore 0:
  9.6 83.0 all-gather.16
  100.1 74.8 all-gather.24
  177.8 73.1 all-gather.26
  252.4 31.3 all-gather.18
  285.2 103.9 all-gather.20
  390.6 104.0 all-gather.22
  616.8 334.4 reduce-scatter.5
  954.1 30.8 reduce-scatter.9
  987.4 99.2 reduce-scatter.13
  1088.8 99.2 reduce-scatter.11
  1191.1 77.0 reduce-scatter.7
  1272.6 235.2 all-reduce.13
where the time goes:
time: 1540 us; the launch traced here: 1530 us
  waiting for transfers between devices  1140 us (74%)
  local copies, waits for them, and re-layouts  119 us (8%)
  blocking collectives  110 us (7%)
  matrix products  105 us (7%)
  other arithmetic  35.4 us (2%)
  between operations  16.4 us (1%)
    reduce_scatter x1, waiting for transfers between devices, shards(): lax.psum_scatter(blocks.reshape(row_count, 2 * width).astype(jnp.bfloat16...  294 us
    psum x1, waiting for transfers between devices, shards(): lax.psum(part_qkv.astype(jnp.bfloat16), 'ctx').astype(jnp.float32)  141 us
    all_gather x1, waiting for transfers between devices, shards(): lax.all_gather(up_weight, 'shard', axis=0, tiled=True)  103 us
    reduce_scatter x1, waiting for transfers between devices, shards(): lax.psum_scatter(grad_down_weight.astype(jnp.bfloat16), 'shard', scatter_...  102 us
    reduce_scatter x1, waiting for transfers between devices, shards(): lax.psum_scatter(grad_up_weight.astype(jnp.bfloat16), 'shard', scatter_di...  101 us
    all_gather x1, waiting for transfers between devices, shards(): lax.all_gather(down_weight, 'shard', axis=0, tiled=True)  97.6 us
    reduce_scatter x1, waiting for transfers between devices, shards(): lax.psum_scatter(grad_qkv_weight.astype(jnp.bfloat16), 'shard', scatter_d...  80.1 us
    all_gather x1, waiting for transfers between devices, shards(): lax.all_gather(qkv_weight, 'shard', axis=0, tiled=True)  71 us
  transfers between devices with their start and end apart: 12, of which 12 were waited for; matrix products, arithmetic and copies ran while one was open for 8% of the time, Pallas kernels for 0%

commit v1 on v0

v1 whole, which is shorter than its diff:
```python
import functools

import jax
import jax.numpy as jnp
from jax import lax
from jax.experimental import pallas as pl
from jax.experimental.pallas import tpu as pltpu
from jax.sharding import PartitionSpec as P

HEADS = 16
F32 = jnp.float32
BF = jnp.bfloat16
neg_large = -1e30
norm_eps = 1e-05
VMEM = 48 * 1024 * 1024


def layer_norm(values, gain_term, bias_term):
    center = values - jnp.mean(values, axis=-1, keepdims=True)
    spread = jnp.mean(center * center, axis=-1, keepdims=True)
    return center * lax.rsqrt(spread + norm_eps) * gain_term + bias_term


def gelu_tanh(values):
    tanh_input = 0.7978845608028654 * (values + 0.044715 * values * values * values)
    return 0.5 * values * (1.0 + jnp.tanh(tanh_input))


def dot(a, b):
    return jnp.dot(a, b, preferred_element_type=F32)


def forward_kernel(block, parts, part_ref, k_ref, qt_ref, vt_ref, ot_ref, lse_ref):
    qi = pl.program_id(0)

    def work():
        qt = qt_ref[...]

        def fold(j, carried, masked):
            top, total, acc = carried
            rows = pl.ds(pl.multiple_of(j * block, block), block)
            s = dot(k_ref[rows, :], qt)
            if masked:
                key = lax.broadcasted_iota(jnp.int32, s.shape, 0)
                query = lax.broadcasted_iota(jnp.int32, s.shape, 1)
                s = jnp.where(key <= query, s, neg_large)
            new_top = jnp.maximum(top, jnp.max(s, axis=0, keepdims=True))
            p = jnp.exp(s - new_top)
            factor = jnp.exp(top - new_top)
            total = total * factor + jnp.sum(p, axis=0, keepdims=True)
            acc = acc * factor + dot(vt_ref[:, rows], p.astype(BF))
            return new_top, total, acc

        start = (
            jnp.full((1, block), neg_large, F32),
            jnp.zeros((1, block), F32),
            jnp.zeros((vt_ref.shape[0], block), F32),
        )
        carried = lax.fori_loop(0, qi, lambda j, c: fold(j, c, False), start)
        top, total, acc = fold(qi, carried, True)
        ot_ref[...] = acc / total
        lse_ref[...] = top + jnp.log(total)

    if parts == 1:
        work()
    else:
        mine = qi % parts == part_ref[0]
        pl.when(mine)(work)

        @pl.when(jnp.logical_not(mine))
        def _():
            ot_ref[...] = jnp.zeros_like(ot_ref)
            lse_ref[...] = jnp.zeros_like(lse_ref)


def backward_kernel(
    block, parts, part_ref, k_ref, kt_ref, v_ref, qt_ref, q_ref, dt_ref, d_ref, dq_ref, dkv_ref
):
    ki = pl.program_id(0)
    width = q_ref.shape[1]

    @pl.when(ki == 0)
    def _():
        dq_ref[...] = jnp.zeros_like(dq_ref)

    dkv_ref[...] = jnp.zeros_like(dkv_ref)

    def step(qi, masked):
        cols = pl.ds(pl.multiple_of(qi * block, block), block)
        s = dot(k_ref[...], qt_ref[:, cols])
        if masked:
            key = lax.broadcasted_iota(jnp.int32, s.shape, 0)
            query = lax.broadcasted_iota(jnp.int32, s.shape, 1)
            s = jnp.where(key <= query, s, neg_large)
        p = jnp.exp(s)
        ds = (p * dot(v_ref[...], dt_ref[:, cols])).astype(BF)
        dkv_ref[:, :width] += dot(ds, q_ref[cols, :])
        dkv_ref[:, width:] += dot(p.astype(BF), d_ref[cols, :])
        dq_ref[:, cols] += dot(kt_ref[...], ds)

    def visit(qi, masked):
        if parts == 1:
            step(qi, masked)
        else:
            pl.when(qi % parts == part_ref[0])(lambda: step(qi, masked))

    visit(ki, True)

    def loop(qi, unused):
        visit(qi, False)
        return unused

    lax.fori_loop(ki + 1, q_ref.shape[0] // block, loop, 0)


def split_bf16(row, count):
    terms = []
    for _ in range(count):
        term = row.astype(BF)
        terms.append(term)
        row = row - term.astype(F32)
    return terms


def whole_spec(shape):
    return pl.BlockSpec(shape, lambda i: (0,) * len(shape))


def attention_forward(part, parts, kaug, qtaug, vt):
    length, depth = kaug.shape
    width = vt.shape[0]
    block = min(512, length)
    return pl.pallas_call(
        functools.partial(forward_kernel, block, parts),
        grid=(length // block,),
        in_specs=[
            pl.BlockSpec(memory_space=pltpu.SMEM),
            whole_spec((length, depth)),
            pl.BlockSpec((depth, block), lambda i: (0, i)),
            whole_spec((width, length)),
        ],
        out_specs=[
            pl.BlockSpec((width, block), lambda i: (0, i)),
            pl.BlockSpec((1, block), lambda i: (0, i)),
        ],
        out_shape=[
            jax.ShapeDtypeStruct((width, length), F32),
            jax.ShapeDtypeStruct((1, length), F32),
        ],
        compiler_params=pltpu.CompilerParams(vmem_limit_bytes=VMEM),
        cost_estimate=pl.CostEstimate(
            flops=8 * length * length * width,
            bytes_accessed=8 * length * width,
            transcendentals=length * length // 2,
        ),
        name="attention_forward",
    )(part, kaug, qtaug, vt)


def attention_backward(part, parts, kaug, kt, vaug, qtaug, q, dtaug, d):
    length, depth = kaug.shape
    width = q.shape[1]
    block = min(512, length)
    return pl.pallas_call(
        functools.partial(backward_kernel, block, parts),
        grid=(length // block,),
        in_specs=[
            pl.BlockSpec(memory_space=pltpu.SMEM),
            pl.BlockSpec((block, depth), lambda i: (i, 0)),
            pl.BlockSpec((width, block), lambda i: (0, i)),
            pl.BlockSpec((block, depth), lambda i: (i, 0)),
            whole_spec((depth, length)),
            whole_spec((length, width)),
            whole_spec((depth, length)),
            whole_spec((length, width)),
        ],
        out_specs=[
            whole_spec((width, length)),
            pl.BlockSpec((block, 2 * width), lambda i: (i, 0)),
        ],
        out_shape=[
            jax.ShapeDtypeStruct((width, length), F32),
            jax.ShapeDtypeStruct((length, 2 * width), F32),
        ],
        compiler_params=pltpu.CompilerParams(vmem_limit_bytes=VMEM),
        cost_estimate=pl.CostEstimate(
            flops=24 * length * length * width,
            bytes_accessed=16 * length * width,
            transcendentals=length * length // 2,
        ),
        name="attention_backward",
    )(part, kaug, kt, vaug, qtaug, q, dtaug, d)


def exchange(pick, shard_count):
    me = lax.axis_index("shard")
    out = [(me, pick(me))]
    for k in range(1, shard_count):
        pairs = [(i, (i + k) % shard_count) for i in range(shard_count)]
        out.append(
            (
                (me - k) % shard_count,
                lax.ppermute(pick((me + k) % shard_count), "shard", pairs),
            )
        )
    return out


def stacked(pieces):
    first = pieces[0][1]
    if len(pieces) == 2:
        me, other = pieces[0][0], pieces[1][1]
        low = jnp.where(me == 0, first, other)
        high = jnp.where(me == 0, other, first)
        return jnp.stack([low, high])
    out = jnp.zeros((len(pieces),) + first.shape, first.dtype)
    for source, piece in pieces:
        out = lax.dynamic_update_index_in_dim(out, piece, source, 0)
    return out


def gather(value, shard_count):
    return stacked(exchange(lambda i: value, shard_count))


def at(value, index, axis):
    return lax.dynamic_index_in_dim(value, index, axis, keepdims=False)


def shards(
    tokens,
    ln1_gain,
    ln1_bias,
    qkv_weight,
    query_bias,
    value_bias,
    dense_weight,
    dense_bias,
    ln2_gain,
    ln2_bias,
    up_weight,
    up_bias,
    down_weight,
    down_bias,
    out_cotangent,
):
    n_shard = lax.axis_size("shard")
    n_ctx = lax.axis_size("ctx")
    me = lax.axis_index("shard")
    local_seqs, rows, width = tokens.shape
    seqs = local_seqs * n_shard
    hd = width // HEADS
    heads = HEADS // n_shard
    half = heads * hd
    length = rows * n_ctx
    total = seqs * rows
    ff = up_bias.shape[0]
    pairs = seqs * heads
    parts = n_ctx // pairs
    assert parts * pairs == n_ctx

    small = jnp.stack([ln1_gain, ln1_bias, dense_bias, ln2_gain, ln2_bias, down_bias])
    small = lax.all_gather(small, "shard", axis=1, tiled=True).astype(F32)
    gain1, shift1, bias_dense, gain2, shift2, bias_down = [small[i] for i in range(6)]
    x_low = gather(tokens, n_shard).reshape(total, width)
    qkv_split = qkv_weight.reshape(half, 3, n_shard, half)
    w_qkv = stacked(exchange(lambda i: at(qkv_split, i, 2), n_shard)).reshape(width, 3 * half)
    w_dense = gather(dense_weight, n_shard).reshape(width, width)
    up_split = up_weight.reshape(half, n_shard, ff)
    w_up = stacked(exchange(lambda i: at(up_split, i, 1), n_shard)).reshape(width, ff)
    g_low = gather(out_cotangent, n_shard).reshape(total, width)

    x = x_low.astype(F32)
    h1 = layer_norm(x, gain1, shift1).astype(BF)
    bias_qkv = jnp.concatenate([query_bias, jnp.zeros_like(query_bias), value_bias])
    qkv = (dot(h1, w_qkv) + bias_qkv.astype(F32)).astype(BF)
    send = (
        qkv.reshape(seqs, rows, 3, heads, hd)
        .transpose(0, 3, 2, 4, 1)
        .reshape(pairs, 1, 3 * hd, rows)
    )

    def to_heads(value):
        value = jnp.broadcast_to(value, (pairs, parts) + value.shape[2:])
        value = value.reshape((n_ctx,) + value.shape[2:])
        value = lax.all_to_all(value, "ctx", split_axis=0, concat_axis=0, tiled=True)
        return value.transpose(1, 0, 2).reshape(value.shape[1], length)

    def from_heads(value):
        value = value.reshape(value.shape[0], n_ctx, rows).transpose(1, 0, 2)
        value = lax.all_to_all(value, "ctx", split_axis=0, concat_axis=0, tiled=True)
        value = value.reshape((pairs, parts) + value.shape[1:])
        if parts > 1:
            return jnp.sum(value.astype(F32), axis=1).astype(BF)
        return value[:, 0]

    mine = lax.axis_index("ctx")
    part = (mine % parts).astype(jnp.int32).reshape(1)
    head = me * heads + (mine // parts) % heads
    order = head.astype(F32)
    slope = jnp.where(
        head < HEADS // 2,
        2.0 ** (-order) / (4.0 * rows),
        2.0 / length * 2.0 ** (-(order - HEADS // 2)),
    )
    qkvt = to_heads(send)
    qt, kt, vt = qkvt[:hd], qkvt[hd : 2 * hd], qkvt[2 * hd :]
    scale = hd**-0.5
    place = jnp.arange(length, dtype=jnp.int32)
    far = (slope * (place - place % 256).astype(F32)).astype(BF)[None]
    near = (slope * (place % 256).astype(F32)).astype(BF)[None]
    one = jnp.ones((1, length), BF)
    fill = jnp.zeros((hd - 5, length), BF)
    kaug = jnp.concatenate([kt, far, near, one, one, one, fill]).T
    qs = (qt.astype(F32) * scale).astype(BF)
    zero = jnp.zeros((1, length), BF)
    ot, lse = attention_forward(
        part, parts, kaug, jnp.concatenate([qs, one, one, zero, zero, zero, fill]), vt
    )

    def to_tokens(value, groups):
        return (
            value.reshape(seqs, heads, groups, hd, rows)
            .transpose(0, 4, 2, 1, 3)
            .reshape(total, groups * half)
        )

    attended_half = to_tokens(from_heads(ot.astype(BF)), 1)
    attended = jnp.moveaxis(gather(attended_half, n_shard), 0, 1).reshape(total, width)

    mid = x + dot(attended, w_dense) + bias_dense
    h2 = layer_norm(mid, gain2, shift2).astype(BF)
    hidden = dot(h2, w_up) + up_bias.astype(F32)
    act = gelu_tanh(hidden).astype(BF)
    out_part = dot(act, down_weight).reshape(n_shard, local_seqs, rows, width)
    out_low = out_part.astype(BF)
    received = exchange(lambda i: at(out_low, i, 0), n_shard)[1:]
    own = lambda value: at(value.reshape(n_shard, local_seqs, rows, width), me, 0)
    block_out = own(mid) + at(out_part, me, 0) + bias_down
    for _, piece in received:
        block_out = block_out + piece.astype(F32)
    block_out = block_out.astype(BF)

    g = g_low.astype(F32)
    grad_down = lax.dot_general(act, g_low, (((0,), (0,)), ((), ())), preferred_element_type=F32)
    d_act = lax.dot_general(
        g_low, down_weight, (((1,), (1,)), ((), ())), preferred_element_type=F32
    )
    d_hidden = jax.vjp(gelu_tanh, hidden)[1](d_act)[0].astype(BF)
    d_h2_part = lax.dot_general(
        d_hidden, w_up, (((1,), (1,)), ((), ())), preferred_element_type=F32
    )
    low = d_h2_part.astype(BF)
    d_h2 = d_h2_part
    for _, piece in exchange(lambda i: low, n_shard)[1:]:
        d_h2 = d_h2 + piece.astype(F32)
    grad_up = lax.dot_general(h2, d_hidden, (((0,), (0,)), ((), ())), preferred_element_type=F32)
    d_mid_norm, grad_gain2, grad_shift2 = jax.vjp(layer_norm, mid, gain2, shift2)[1](d_h2)
    d_mid = g + d_mid_norm
    d_dense = d_mid.astype(BF)
    d_attended = lax.dot_general(
        d_dense, dense_weight, (((1,), (1,)), ((), ())), preferred_element_type=F32
    ).astype(BF)
    grad_dense = lax.dot_general(
        attended_half, d_dense, (((0,), (0,)), ((), ())), preferred_element_type=F32
    )

    dt = to_heads(
        d_attended.reshape(seqs, rows, heads, hd)
        .transpose(0, 2, 3, 1)
        .reshape(pairs, 1, hd, rows)
    )
    delta = jnp.sum(dt.astype(F32) * ot, axis=0, keepdims=True)
    qtaug = jnp.concatenate([qs, one, one] + split_bf16(-lse, 3) + [fill])
    dtaug = jnp.concatenate([dt] + split_bf16(-delta, 3) + [jnp.zeros((hd - 3, length), BF)])
    vaug = jnp.concatenate([vt, one, one, one, jnp.zeros((hd - 3, length), BF)]).T
    dqt, dkv = attention_backward(part, parts, kaug, kt, vaug, qtaug, qs.T, dtaug, dt.T)
    d_qkvt = jnp.concatenate([(dqt * scale).astype(BF), dkv.astype(BF).T])
    d_qkv = to_tokens(from_heads(d_qkvt), 3)

    grad_qkv = lax.dot_general(h1, d_qkv, (((0,), (0,)), ((), ())), preferred_element_type=F32)
    d_h1_part = lax.dot_general(d_qkv, w_qkv, (((1,), (1,)), ((), ())), preferred_element_type=F32)
    _, grad_gain1, grad_shift1 = jax.vjp(layer_norm, x, gain1, shift1)[1](d_h1_part)
    d_h1_split = d_h1_part.reshape(n_shard, local_seqs, rows, width)
    d_h1_low = d_h1_split.astype(BF)
    d_h1 = at(d_h1_split, me, 0)
    for _, piece in exchange(lambda i: at(d_h1_low, i, 0), n_shard)[1:]:
        d_h1 = d_h1 + piece.astype(F32)
    d_x = jax.vjp(layer_norm, own(x), gain1, shift1)[1](d_h1)[0]
    input_grad = (own(d_mid) + d_x).astype(BF)

    def column(value, count):
        value = jnp.sum(value.astype(F32), axis=0)
        return lax.dynamic_slice_in_dim(value, me * count, count, 0)

    def piece(value):
        return lax.dynamic_slice_in_dim(value, me * half, half, 0)

    sum_down = lax.psum(grad_down.astype(BF), "ctx")
    sum_up = lax.psum(grad_up.astype(BF), "ctx")
    sum_dense = lax.psum(grad_dense.astype(BF), "ctx")
    sum_down, sum_up, sum_dense, grad_qkv = lax.optimization_barrier(
        (sum_down, sum_up, sum_dense, grad_qkv.astype(BF))
    )
    sum_down, sum_dense = sum_down.astype(F32), sum_dense.astype(F32)
    sum_up = sum_up.reshape(n_shard, half, ff)
    sum_up = stacked(exchange(lambda i: at(sum_up, i, 0), n_shard))
    sum_up = jnp.moveaxis(sum_up, 0, 1).reshape(half, n_shard * ff).astype(F32)
    sum_qkv = lax.psum(grad_qkv, "ctx")
    sum_qkv = sum_qkv.reshape(n_shard, half, 3, half)
    sum_qkv = stacked(exchange(lambda i: at(sum_qkv, i, 0), n_shard))
    sum_qkv = sum_qkv.transpose(1, 2, 0, 3).reshape(half, 3 * width).astype(F32)

    d_qkv_sum = jnp.sum(d_qkv.astype(F32), axis=0)
    early = jnp.concatenate(
        [
            column(g, half),
            jnp.sum(d_hidden.astype(F32), axis=0),
            piece(grad_gain2),
            piece(grad_shift2),
            column(d_dense, half),
        ]
    )
    early = lax.psum(early, "ctx")
    blank = jnp.zeros((width,), F32)
    late = jnp.stack(
        [
            grad_gain1,
            grad_shift1,
            lax.dynamic_update_slice_in_dim(blank, d_qkv_sum[:half], me * half, 0),
            lax.dynamic_update_slice_in_dim(blank, d_qkv_sum[2 * half :], me * half, 0),
        ]
    )
    late = lax.psum(late, ("shard", "ctx"))
    late = lax.dynamic_slice_in_dim(late, me * half, half, 1)
    cut = [half, half + ff, 2 * half + ff, 3 * half + ff]
    down_bias_sum, up_bias_sum, gain2_sum, shift2_sum, dense_bias_sum = jnp.split(early, cut)
    return (
        block_out,
        input_grad,
        late[0],
        late[1],
        sum_qkv,
        late[2],
        late[3],
        sum_dense,
        dense_bias_sum,
        gain2_sum,
        shift2_sum,
        sum_up,
        up_bias_sum,
        sum_down,
        down_bias_sum,
    )


def solution(mesh):
    return jax.shard_map(
        shards,
        mesh=mesh,
        in_specs=(
            P("shard", "ctx", None),
            P("shard"),
            P("shard"),
            P("shard", None),
            P("shard"),
            P("shard"),
            P("shard", None),
            P("shard"),
            P("shard"),
            P("shard"),
            P("shard", None),
            P("shard"),
            P("shard", None),
            P("shard"),
            P("shard", "ctx", None),
        ),
        out_specs=(
            P("shard", "ctx", None),
            P("shard", "ctx", None),
            P("shard"),
            P("shard"),
            P("shard", None),
            P("shard"),
            P("shard"),
            P("shard", None),
            P("shard"),
            P("shard"),
            P("shard"),
            P("shard", None),
            P("shard"),
            P("shard", None),
            P("shard"),
        ),
        check_vma=False,
    )
```

time: 1540 us -> 748 us (0.49)
  waiting for transfers between devices: 1140 us -> 136 us
  blocking collectives: 110 us -> 188 us
  local copies, waits for them, and re-layouts: 119 us -> 193 us
  matrix products: 105 us -> 45.1 us
  Pallas kernels: 0 us -> 55.5 us
  other arithmetic: 35.4 us -> 73 us
  starting transfers between devices: 0.69 us -> 34.1 us
    reduce_scatter x5 -> x0, waiting for transfers between devices: 605 us -> none  [the longest x1 294 us: shards(): lax.psum_scatter(blocks.reshape(row_count, 2 * width).astype(jnp.bfloat16...]
    all_gather x6 -> x0, waiting for transfers between devices: 388 us -> none  [the longest x1 103 us: shards(): lax.all_gather(up_weight, 'shard', axis=0, tiled=True)]
    psum x1 -> x2, waiting for transfers between devices: 141 us -> 26.5 us  [the longest x1 18.9 us: shards(): sum_down = lax.psum(grad_down.astype(BF), 'ctx')]
    ppermute x0 -> x11, waiting for transfers between devices: none -> 98.5 us  [exchange(): lax.ppermute(pick((me + k) % shard_count), 'shard', pairs)]
    psum x1 -> x2, blocking collectives: 62.4 us -> 157 us  [the longest x1 86.5 us: shards(): late = lax.psum(late, ('shard', 'ctx'))]
    dot_general x19 -> x12, matrix products: 105 us -> 45.1 us  [the longest x4 14.4 us: dot(): return jnp.dot(a, b, preferred_element_type=F32)]
    pallas_call x0 -> x2, Pallas kernels: none -> 55.5 us  [the longest x1 32.7 us: attention_backward(): pl.pallas_call(functools.partial(backward_kernel, block, parts), grid=(le...]
    dynamic_update_slice x16 -> x2, local copies, waits for them, and re-layouts: 35.3 us -> 0.02 us  [the longest x1 0.01 us: shards(): lax.dynamic_update_slice_in_dim(blank, d_qkv_sum[:half], me * half, 0)]
  transfers between devices with their start and end apart: 12 -> 17, of which waited for: 12 -> 8; matrix products, arithmetic and copies ran while one was open for 8% -> 28% of each run, Pallas kernels for 0% -> 4%
where the time goes in v1:
time: 748 us; the launch traced here: 739 us
  local copies, waits for them, and re-layouts  193 us (26%)
  blocking collectives  188 us (25%)
  waiting for transfers between devices  136 us (18%)
  other arithmetic  73 us (10%)
  Pallas kernels  55.5 us (7%)
  matrix products  45.1 us (6%)
  starting transfers between devices  34.1 us (5%)
  between operations  15.4 us (2%)
    ppermute x11, waiting for transfers between devices, exchange(): lax.ppermute(pick((me + k) % shard_count), 'shard', pairs)  98.5 us
    psum x1, blocking collectives, shards(): late = lax.psum(late, ('shard', 'ctx'))  86.5 us
    psum x1, blocking collectives, shards(): early = lax.psum(early, 'ctx')  70.8 us
    unnamed x123, local copies, waits for them, and re-layouts  47.3 us
    dynamic_slice x9, local copies, waits for them, and re-layouts, at(): return lax.dynamic_index_in_dim(value, index, axis, keepdims=False)  43.8 us
    pallas_call x1, Pallas kernels, attention_backward(): pl.pallas_call(functools.partial(backward_kernel, block, parts), grid=(le...  32.7 us
    all_gather x1, blocking collectives, shards(): small = lax.all_gather(small, 'shard', axis=1, tiled=True).astype(F32)  30.3 us
    another operation x11, other arithmetic, stacked(): return jnp.stack([low, high])  24 us
  transfers between devices with their start and end apart: 17, of which 8 were waited for; matrix products, arithmetic and copies ran while one was open for 28% of the time, Pallas kernels for 4%

profile of v1, /device:TPU:0, one launch (start us, length us, event | category | flops | bytes accessed | tf_op | source)
XLA Modules:
  0.0 739.4 jit_solution(2851119331527195673)
XLA Ops:
  7.2 3.0 collective-permute-start
  10.2 4.6 copy.167
  14.9 2.2 constant_dynamic-slice_fusion.6
  18.7 6.5 copy.187
  26.0 30.3 %all_gather.3 = bf16[6,1024]{1,0:T(8,128)(2,1)S(1)} all-gather(bf16[6,512]{1,0:T(8,128)(2,1)S(1)} %stack.113), channel_id=1, replica_groups=mesh['ctx'=16,'shard'=2] {'shard'}, dimensions={1}, use_global_device_ids=true | all-gather | bytes 18432 | tf_op jit(solution)/shard_map/all_gather | solution.py:263
  63.3 8.7 %copy.170 = bf16[2,512,3,512]{1,0,3,2:T(2,128)(2,1)} copy(bf16[2,512,3,512]{3,1,2,0:T(8,128)(2,1)} %pad_maximum_fusion.1) | data formatting | bytes 6291456 | tf_op jit(solution)/shard_map/stack | solution.py:215
  72.0 2.8 copy.217
  76.5 3.0 fusion.8
  83.1 2.9 copy.172
  85.9 6.3 all-to-all-start
  92.3 4.5 constant_dynamic-slice_fusion.4
  96.8 4.0 copy.189
  104.3 3.9 copy.188
  108.5 52.2 %collective-permute-done.6 = bf16[1,256,1024]{2,1,0:T(8,128)(2,1)} collective-permute-done((bf16[1,256,1024]{2,1,0:T(8,128)(2,1)S(1)}, bf16[1,256,1024]{2,1,0:T(8,128)(2,1)}, u32[]{:S(2)}, u32[]{:S(2)}) %collective-permute-start.6) | collective-permute-done | bytes 524320 | tf_op jit(solution)/shard_map/ppermute | solution.py:203
  165.9 16.9 %collective-permute-done.3 = bf16[512,1024]{1,0:T(8,128)(2,1)} collective-permute-done((bf16[512,1024]{1,0:T(8,128)(2,1)}, bf16[512,1024]{1,0:T(8,128)(2,1)}, u32[]{:S(2)}, u32[]{:S(2)}) %collective-permute-start.3) | collective-permute-done | bytes 1048608 | tf_op jit(solution)/shard_map/ppermute | solution.py:203
  182.8 2.7 select_bitcast_fusion.1
  185.5 4.1 fusion.15
  203.0 22.8 %attention_forward.1 = (f32[64,4096]{1,0:T(8,128)S(1)}, f32[1,4096]{1,0:T(1,128)S(1)}) custom-call(s32[1]{0:T(128)} %constant.155.clone.1.part_ref, bf16[4096,128]{1,0:T(8,128)(2,1)S(1)} %copy-done, bf16[128,4096]{1,0:T(8,128)(2,1)S(1)} %copy-done.4, bf16[64,4096]{1,0:T(8,128)(2,1)S(1)} %copy.180.vt_ref), custom_call_target="tpu_custom_call" | custom-call | flops 8589934592 | bytes 2097152 | tf_op jit(solution)/shard_map/attention_forward/pallas_call | solution.py:133
  226.8 6.0 all-to-all-start.1
  232.8 4.6 pad_maximum_fusion
  241.4 5.8 all-to-all-done.1
  250.4 3.9 subtract_convert_fusion.1
  256.8 6.9 concatenate.54
  263.7 2.4 copy.202.qt_ref
  267.7 2.7 fusion.64
  270.9 2.4 fusion.52
  273.7 6.2 convert_reduce_fusion
  279.9 2.4 fusion.65
  285.6 4.6 convolution_convert_fusion.1
  290.2 17.0 %collective-permute-done.7 = bf16[512,1024]{1,0:T(8,128)(2,1)S(1)} collective-permute-done((bf16[512,1024]{1,0:T(8,128)(2,1)S(1)}, bf16[512,1024]{1,0:T(8,128)(2,1)S(1)}, u32[]{:S(2)}, u32[]{:S(2)}) %collective-permute-start.7) | collective-permute-done | bytes 1048608 | tf_op jit(solution)/shard_map/ppermute | solution.py:203
  318.0 4.4 all-to-all-start.2
  322.7 7.6 %convolution_convert_fusion.2 = bf16[2048,1024]{1,0:T(8,128)(2,1)} fusion(bf16[512,1024]{1,0:T(8,128)(2,1)S(1)} %bitcast.262, f32[512,2048]{1,0:T(8,128)} %copy-done.54, f32[2048]{0:T(1024)S(1)} %convert_element_type.354), kind=kOutput, calls=%fused_computation.18 | convolution fusion | flops 2160066560 | bytes 9445376 | tf_op jit(solution)/shard_map/dot_general | solution.py:345
  332.1 4.9 all-to-all-done.2
  338.6 2.6 multiply_reduce_fusion.1
  346.7 3.9 subtract_convert_fusion
  350.6 6.6 concatenate.55
  357.2 2.3 copy.203.dt_ref
  363.2 32.7 %attention_backward.1 = (f32[64,4096]{1,0:T(8,128)S(1)}, f32[4096,128]{1,0:T(8,128)}) custom-call(s32[1]{0:T(128)} %constant.155.clone.1.part_ref, bf16[4096,128]{1,0:T(8,128)(2,1)S(1)} %copy-done.1, bf16[64,4096]{1,0:T(8,128)(2,1)S(1)} %bitcast.234, bf16[4096,128]{1,0:T(8,128)(2,1)S(1)} %copy-done.3, bf16[128,4096]{1,0:T(8,128)(2,1)S(1)} %copy-done.2, ...), custom_call_target="tpu_custom_call" | custom-call | flops 25769803776 | bytes 4194304 | tf_op jit(solution)/shard_map/attention_backward/pallas_call | solution.py:164
  401.4 2.3 pad_maximum_fusion.2
  403.6 3.9 copy.206
  407.5 4.5 all-to-all-start.3
  412.3 6.3 fusion.54
  422.0 12.4 %collective-permute-done.5 = bf16[1,256,1024]{2,1,0:T(8,128)(2,1)} collective-permute-done((bf16[1,256,1024]{2,1,0:T(8,128)(2,1)S(1)}, bf16[1,256,1024]{2,1,0:T(8,128)(2,1)}, u32[]{:S(2)}, u32[]{:S(2)}) %collective-permute-start.5) | collective-permute-done | bytes 524320 | tf_op jit(solution)/shard_map/ppermute | solution.py:203
  434.4 2.5 fusion.38
  437.1 70.8 %psum.47 = f32[4096]{0:T(1024)S(1)} all-reduce(f32[4096]{0:T(1024)S(1)} %constant_dynamic-update-slice_fusion.2), channel_id=1, replica_groups=mesh['ctx'=16,'shard'=2] {'ctx'}, use_global_device_ids=true, to_apply=%region_24.25 | all-reduce | flops 4096 | bytes 32768 | tf_op jit(solution)/shard_map/psum | solution.py:424
  512.0 3.5 convolution_convert_fusion
  515.5 3.2 fusion.20
  518.7 18.9 %all-reduce.6.cloned.1.call-done = (bf16[2048,1024]{1,0:T(8,128)(2,1)}, bf16[1024,2048]{1,0:T(8,128)(2,1)}, bf16[512,1024]{1,0:T(8,128)(2,1)}) async-done(((bf16[2048,1024]{1,0:T(8,128)(2,1)}, bf16[1024,2048]{1,0:T(8,128)(2,1)}, bf16[512,1024]{1,0:T(8,128)(2,1)}), (bf16[2048,1024]{1,0:T(8,128)(2,1)}, bf16[1024,2048]{1,0:T(8,128)(2,1)}, bf16[512,1024]{1,0:T(8,128)(2,1)})) %all-reduce.6.cloned.1.call-update) | async-done | bytes 9437200 | tf_op jit(solution)/shard_map/psum | solution.py:399
  537.6 4.6 copy.208
  542.3 6.1 reshape.832
  551.8 3.2 dynamic-slice_bitcast_fusion
  555.5 86.5 %psum.42 = f32[4,1024]{1,0:T(4,128)S(1)} all-reduce(f32[4,1024]{1,0:T(4,128)S(1)} %pad_maximum_fusion.6), channel_id=1, replica_groups=mesh['ctx'=16,'shard'=2] {'shard','ctx'}, use_global_device_ids=true, to_apply=%region_14.15 | all-reduce | flops 4096 | bytes 32768 | tf_op jit(solution)/shard_map/psum | solution.py:434
  644.8 7.6 %all-reduce.4.cloned.1.call-done = bf16[2,512,3,512]{1,0,3,2:T(2,128)(2,1)} async-done(((bf16[2,512,3,512]{1,0,3,2:T(2,128)(2,1)}), bf16[2,512,3,512]{1,0,3,2:T(2,128)(2,1)}) %all-reduce.4.cloned.1.call-update) | async-done | bytes 3145744 | tf_op jit(solution)/shard_map/psum | solution.py:409
  652.4 12.0 %constant_dynamic-slice_fusion.2 = (bf16[1,512,3,512]{1,0,3,2:T(2,128)(2,1)}, bf16[1,512,3,512]{1,0,3,2:T(2,128)(2,1)}) fusion(bf16[2,512,3,512]{1,0,3,2:T(2,128)(2,1)} %all-reduce.4.cloned.1.call-done, s32[]{:T(128)S(6)} %select_n.173, s32[]{:T(128)S(6)} %select_n.175), kind=kLoop, calls=%fused_computation.122 | loop fusion | bytes 6291464 | tf_op jit(solution)/shard_map/jit(dynamic_index_in_dim)/dynamic_slice | solution.py:227
  664.4 8.2 %copy.210 = bf16[1,512,3,512]{3,1,2,0:T(8,128)(2,1)} copy(bf16[1,512,3,512]{1,0,3,2:T(2,128)(2,1)} %get-tuple-element.109) | data formatting | bytes 3145728 | tf_op jit(solution)/shard_map/jit(dynamic_index_in_dim)/dynamic_slice | solution.py:227
  678.9 4.4 convert_element_type.396
  683.3 6.8 copy.209
  690.1 2.5 fusion.13
  692.6 3.9 convert_bitcast_fusion
  696.6 8.8 %copy.212 = f32[512,2,2048]{0,2,1:T(8,128)} copy(f32[512,2,2048]{2,0,1:T(8,128)} %convert_bitcast_fusion) | data formatting | bytes 16777216 | tf_op jit(solution)/shard_map/convert_element_type | solution.py:408
  705.3 8.9 %copy.214 = f32[512,4096]{1,0:T(8,128)} copy(f32[512,4096]{0,1:T(8,128)} %bitcast.235) | data formatting | bytes 16777216
  715.9 3.1 convert_bitcast_fusion.1
  719.0 6.6 copy.211
  725.5 6.6 copy.213
  (248 shorter events, 104.4 us)
Async XLA Ops:
  7.2 49.2 %collective-permute-start = (bf16[1,256,1024]{2,1,0:T(8,128)(2,1)}, bf16[1,256,1024]{2,1,0:T(8,128)(2,1)}, u32[]{:S(2)}, u32[]{:S(2)}) collective-permute-start(bf16[1,256,1024]{2,1,0:T(8,128)(2,1)} %param.15), channel_id=1, source_target_pairs={{0,1},{1,0},{2,3},{3,2},{4,5},{5,4},{6,7},{7,6},{8,9},{9,8},{10,11... | collective-permute-start | bytes 1572872 | tf_op jit(solution)/shard_map/ppermute | solution.py:203
  18.6 41.1 %collective-permute-start.1 = (bf16[512,3,512]{2,0,1:T(8,128)(2,1)}, bf16[512,3,512]{2,0,1:T(8,128)(2,1)}, u32[]{:S(2)}, u32[]{:S(2)}) collective-permute-start(bf16[512,3,512]{2,0,1:T(8,128)(2,1)} %bitcast.275), channel_id=1, source_target_pairs={{0,1},{1,0},{2,3},{3,2},{4,5},{5,4},{6,7},{7,6},{8,9},{9,8},{10,11... | collective-permute-start | bytes 4718600 | tf_op jit(solution)/shard_map/ppermute | solution.py:203
  18.6 6.5 copy-start.45
  18.6 6.5 copy-start.46
  18.6 6.5 copy-start.47
  18.6 6.6 copy-start.48
  18.6 6.6 copy-start.49
  18.7 6.6 copy-start.50
  25.1 31.1 %copy-start.51 = (bf16[512]{0:T(512)(128)(2,1)S(1)}, bf16[512]{0:T(512)(128)(2,1)}, u32[]{:S(2)}) copy-start(bf16[512]{0:T(512)(128)(2,1)} %param.20) | copy-start | bytes 3076
  25.1 31.1 %copy-start.52 = (bf16[512]{0:T(512)(128)(2,1)S(1)}, bf16[512]{0:T(512)(128)(2,1)}, u32[]{:S(2)}) copy-start(bf16[512]{0:T(512)(128)(2,1)} %param.19) | copy-start | bytes 3076
  56.3 2.0 copy-start.42
  57.6 106.3 %copy-start.9 = (bf16[1,1,256,1024]{3,2,1,0:T(8,128)(2,1)}, bf16[1,1,256,1024]{3,2,1,0:T(8,128)(2,1)S(1)}, u32[]{:S(2)}) copy-start(bf16[1,1,256,1024]{3,2,1,0:T(8,128)(2,1)S(1)} %get-tuple-element.124) | copy-start | bytes 1572868
  57.6 106.3 %copy-start.11 = (bf16[1,1,256,1024]{3,2,1,0:T(8,128)(2,1)}, bf16[1,1,256,1024]{3,2,1,0:T(8,128)(2,1)S(1)}, u32[]{:S(2)}) copy-start(bf16[1,1,256,1024]{3,2,1,0:T(8,128)(2,1)S(1)} %get-tuple-element.125) | copy-start | bytes 1572868
  72.0 4.5 copy-start.39
  74.9 1.6 copy-start.29
  85.9 103.7 %all-to-all-start = ((bf16[16,192,256]{2,1,0:T(8,128)(2,1)}), bf16[16,192,256]{2,1,0:T(8,128)(2,1)S(1)}, u32[]{:S(2)}, u32[]{:S(2)}) async-start(bf16[16,192,256]{2,1,0:T(8,128)(2,1)} %bitcast.251), calls=%async_computation | async-start | bytes 3145728 | tf_op jit(solution)/shard_map/all_to_all | solution.py:286
  96.8 5.5 copy-start.41
  100.7 84.8 %collective-permute-start.4 = (bf16[512,2048]{1,0:T(8,128)(2,1)}, bf16[512,2048]{1,0:T(8,128)(2,1)}, u32[]{:S(2)}, u32[]{:S(2)}) collective-permute-start(bf16[512,2048]{1,0:T(8,128)(2,1)} %bitcast.269), channel_id=1, source_target_pairs={{0,1},{1,0},{2,3},{3,2},{4,5},{5,4},{6,7},{7,6},{8,9},{9,8},{10,11... | collective-permute-start | bytes 6291464 | tf_op jit(solution)/shard_map/ppermute | solution.py:203
  102.3 58.5 %collective-permute-start.6 = (bf16[1,256,1024]{2,1,0:T(8,128)(2,1)S(1)}, bf16[1,256,1024]{2,1,0:T(8,128)(2,1)}, u32[]{:S(2)}, u32[]{:S(2)}) collective-permute-start(bf16[1,256,1024]{2,1,0:T(8,128)(2,1)S(1)} %copy-done.41), channel_id=1, source_target_pairs={{0,1},{1,0},{2,3},{3,2},{4,5},{5,4},{6,7},{7,6},{8,9},{9,8},{10,11... | collective-permute-start | bytes 1572872 | tf_op jit(solution)/shard_map/ppermute | solution.py:203
  102.8 80.0 %collective-permute-start.3 = (bf16[512,1024]{1,0:T(8,128)(2,1)}, bf16[512,1024]{1,0:T(8,128)(2,1)}, u32[]{:S(2)}, u32[]{:S(2)}) collective-permute-start(bf16[512,1024]{1,0:T(8,128)(2,1)} %param.21), channel_id=1, source_target_pairs={{0,1},{1,0},{2,3},{3,2},{4,5},{5,4},{6,7},{7,6},{8,9},{9,8},{10,11... | collective-permute-start | bytes 3145736 | tf_op jit(solution)/shard_map/ppermute | solution.py:203
  104.3 4.0 copy-start.44
  162.0 3.9 copy-start.20
  163.9 18.9 %copy-start.25 = (bf16[512,1024]{1,0:T(8,128)(2,1)S(1)}, bf16[512,1024]{1,0:T(8,128)(2,1)}, u32[]{:S(2)}) copy-start(bf16[512,1024]{1,0:T(8,128)(2,1)} %param.21) | copy-start | bytes 3145732
  165.9 19.6 %copy-start.19 = (bf16[512,1,2048]{2,0,1:T(8,128)(2,1)S(1)}, bf16[512,1,2048]{2,0,1:T(8,128)(2,1)}, u32[]{:S(2)}) copy-start(bf16[512,1,2048]{2,0,1:T(8,128)(2,1)} %copy.188) | copy-start | bytes 6291460
  191.5 2.3 copy-start.32
  197.5 1.3 copy-start.33
  226.8 20.5 %all-to-all-start.1 = ((bf16[16,64,256]{2,1,0:T(8,128)(2,1)}), bf16[16,64,256]{2,1,0:T(8,128)(2,1)S(1)}, u32[]{:S(2)}, u32[]{:S(2)}) async-start(bf16[16,64,256]{2,1,0:T(8,128)(2,1)} %bitcast.272), calls=%async_computation.1 | async-start | bytes 1048576 | tf_op jit(solution)/shard_map/all_to_all | solution.py:291
  248.9 17.2 %collective-permute-start.2 = (bf16[512,512]{1,0:T(8,128)(2,1)}, bf16[512,512]{1,0:T(8,128)(2,1)}, u32[]{:S(2)}, u32[]{:S(2)}) collective-permute-start(bf16[512,512]{1,0:T(8,128)(2,1)} %copy.184), channel_id=1, source_target_pairs={{0,1},{1,0},{2,3},{3,2},{4,5},{5,4},{6,7},{7,6},{8,9},{9,8},{10,11... | collective-permute-start | bytes 1572872 | tf_op jit(solution)/shard_map/ppermute | solution.py:203
  263.6 2.4 copy-start.31
  266.0 1.4 copy-start.37
  266.1 1.7 copy-start.38
  267.7 3.1 copy-start.27
  270.5 37.6 %copy-start.8 = (f32[512,1024]{1,0:T(8,128)}, f32[512,1024]{1,0:T(8,128)S(1)}, u32[]{:S(2)}) copy-start(f32[512,1024]{1,0:T(8,128)S(1)} %get-tuple-element.150) | copy-start | bytes 6291460
  270.9 2.5 copy-start.28
  270.9 2.9 copy-start.53
  273.3 6.6 copy-start.54
  279.9 4.1 copy-start.16
  282.3 24.9 %collective-permute-start.7 = (bf16[512,1024]{1,0:T(8,128)(2,1)S(1)}, bf16[512,1024]{1,0:T(8,128)(2,1)S(1)}, u32[]{:S(2)}, u32[]{:S(2)}) collective-permute-start(bf16[512,1024]{1,0:T(8,128)(2,1)S(1)} %get-tuple-element.151), channel_id=1, source_target_pairs={{0,1},{1,0},{2,3},{3,2},{4,5},{5,4},{6,7},{7,6},{8,9},{9,8},{10,11... | collective-permute-start | bytes 3145736 | tf_op jit(solution)/shard_map/ppermute | solution.py:203
  308.8 1.7 copy-start.26
  309.3 1.3 copy-start.5
  318.0 19.0 %all-to-all-start.2 = ((bf16[16,64,256]{2,1,0:T(8,128)(2,1)}), bf16[16,64,256]{2,1,0:T(8,128)(2,1)}, u32[]{:S(2)}, u32[]{:S(2)}) async-start(bf16[16,64,256]{2,1,0:T(8,128)(2,1)} %bitcast.271), calls=%async_computation.2 | async-start | bytes 1048576 | tf_op jit(solution)/shard_map/all_to_all | solution.py:286
  322.5 215.2 %all-reduce.6.cloned.1.call-start = ((), (), s32[]{:S(2)}) async-start(), calls=%async_computation.5 | async-start | bytes 18874368 | tf_op jit(solution)/shard_map/psum | solution.py:399
  322.7 7.6 %copy-start.6 = (f32[512,1024]{1,0:T(8,128)S(1)}, f32[512,1024]{1,0:T(8,128)}, u32[]{:S(2)}) copy-start(f32[512,1024]{1,0:T(8,128)} %copy-done.5) | copy-start | bytes 6291460
  338.6 12.0 %copy-start.17 = (bf16[64,16,256]{0,2,1:T(8,128)(2,1)}, bf16[64,16,256]{0,2,1:T(8,128)(2,1)S(1)}, u32[]{:S(2)}) copy-start(bf16[64,16,256]{0,2,1:T(8,128)(2,1)S(1)} %copy.196) | copy-start | bytes 1572868
  360.7 1.3 copy-start.2
  362.0 1.2 copy-start.3
  407.5 101.6 %all-to-all-start.3 = ((bf16[16,192,256]{2,1,0:T(8,128)(2,1)}), bf16[16,192,256]{2,1,0:T(8,128)(2,1)S(1)}, u32[]{:S(2)}, u32[]{:S(2)}) async-start(bf16[16,192,256]{2,1,0:T(8,128)(2,1)} %bitcast.57), calls=%async_computation.3 | async-start | bytes 3145728 | tf_op jit(solution)/shard_map/all_to_all | solution.py:291
  412.0 240.3 %all-reduce.4.cloned.1.call-start = ((), (), s32[]{:S(2)}) async-start(), calls=%async_computation.4 | async-start | bytes 6291456 | tf_op jit(solution)/shard_map/psum | solution.py:409
  418.6 1.3 copy-start.34
  418.6 3.1 copy-start.21
  418.6 3.1 copy-start.23
  420.0 14.4 %collective-permute-start.5 = (bf16[1,256,1024]{2,1,0:T(8,128)(2,1)S(1)}, bf16[1,256,1024]{2,1,0:T(8,128)(2,1)}, u32[]{:S(2)}, u32[]{:S(2)}) collective-permute-start(bf16[1,256,1024]{2,1,0:T(8,128)(2,1)S(1)} %fusion.39), channel_id=1, source_target_pairs={{0,1},{1,0},{2,3},{3,2},{4,5},{5,4},{6,7},{7,6},{8,9},{9,8},{10,11... | collective-permute-start | bytes 1572872 | tf_op jit(solution)/shard_map/ppermute | solution.py:203
  420.2 14.2 %copy-start.35 = (f32[512,1024]{1,0:T(8,128)S(1)}, f32[512,1024]{1,0:T(8,128)}, u32[]{:S(2)}) copy-start(f32[512,1024]{1,0:T(8,128)} %copy-done.34) | copy-start | bytes 6291460
  510.8 1.2 copy-start.40
  512.0 3.5 copy-start.10
  512.0 3.5 copy-start.12
  512.0 3.5 copy-start.30
  549.7 93.0 %collective-permute-start.8 = (bf16[1,256,1024]{2,1,0:T(8,128)(2,1)S(1)}, bf16[1,256,1024]{2,1,0:T(8,128)(2,1)S(1)}, u32[]{:S(2)}, u32[]{:S(2)}) collective-permute-start(bf16[1,256,1024]{2,1,0:T(8,128)(2,1)S(1)} %fusion.40), channel_id=1, source_target_pairs={{0,1},{1,0},{2,3},{3,2},{4,5},{5,4},{6,7},{7,6},{8,9},{9,8},{10,11... | collective-permute-start | bytes 1572872 | tf_op jit(solution)/shard_map/ppermute | solution.py:203
  551.8 91.0 %copy-start.43 = (f32[1,1024]{1,0:T(1,128)S(1)}, f32[1,1024]{1,0:T(1,128)}, u32[]{:S(2)}) copy-start(f32[1,1024]{1,0:T(1,128)} %copy-done.42) | copy-start | bytes 12292
  554.9 135.2 %collective-permute-start.10 = (bf16[512,2048]{1,0:T(8,128)(2,1)}, bf16[512,2048]{1,0:T(8,128)(2,1)}, u32[]{:S(2)}, u32[]{:S(2)}) collective-permute-start(bf16[512,2048]{1,0:T(8,128)(2,1)} %dynamic-slice_bitcast_fusion), channel_id=1, source_target_pairs={{0,1},{1,0},{2,3},{3,2},{4,5},{5,4},{6,7},{7,6},{8,9},{9,8},{10,11... | collective-permute-start | bytes 6291464 | tf_op jit(solution)/shard_map/ppermute | solution.py:203
  672.6 3.4 copy-start.7
  672.6 41.7 %collective-permute-start.9 = (bf16[512,3,512]{2,0,1:T(8,128)(2,1)}, bf16[512,3,512]{2,0,1:T(8,128)(2,1)}, u32[]{:S(2)}, u32[]{:S(2)}) collective-permute-start(bf16[512,3,512]{2,0,1:T(8,128)(2,1)} %bitcast.70), channel_id=1, source_target_pairs={{0,1},{1,0},{2,3},{3,2},{4,5},{5,4},{6,7},{7,6},{8,9},{9,8},{10,11... | collective-permute-start | bytes 4718600 | tf_op jit(solution)/shard_map/ppermute | solution.py:203
  675.9 1.4 copy-start.36
  675.9 3.0 copy-start.24
  (8 other events, 8.4 us)
Sparse Core Ops, SparseCore 0:
  332.2 205.3 all-reduce.5
  548.6 103.7 all-reduce.3
